TPU v7x, 32 devices: a whole 2x2x4 slice. The times are simulated.
32 devices in a mesh: groups: 2 (over y), seq: 4 (over z), mp: 2 (over x), rep: 2 (over core).
Axes of the slice: x: 2, y: 2, z: 4, core: 2. Of those that a mesh axis runs over, the one named last changes fastest.
Arguments:
- query_states: bfloat16 [8, 512, 2048], P(('groups', 'mp', 'rep'), 'seq'), parts along dimension 0, may hold values from -10 to 10
- key_states: bfloat16 [8, 512, 2048], P(('groups', 'mp', 'rep'), 'seq'), parts along dimension 0, may hold values from -10 to 10
- value_states: bfloat16 [8, 512, 2048], P(('groups', 'mp', 'rep'), 'seq'), parts along dimension 0, may hold values from -6 to 6
- out_grad: bfloat16 [8, 512, 2048], P(('groups', 'mp', 'rep'), 'seq'), parts along dimension 0, may hold values from -12 to 12
- pattern: int32 [16, 4, 6], P('seq'), may hold values from 0 to 3, as said below
- counts: int32 [16, 4], P('seq'), may hold values from 1 to 6, as said below
Outputs:
- query_grad: bfloat16 [8, 512, 2048], P(('groups', 'mp', 'rep'), 'seq'), parts along dimension 0
- key_grad: bfloat16 [8, 512, 2048], P(('groups', 'mp', 'rep'), 'seq'), parts along dimension 0
- value_grad: bfloat16 [8, 512, 2048], P(('groups', 'mp', 'rep'), 'seq'), parts along dimension 0
There are 2 independent parts, one for each index of `groups`. A program takes and returns all parts, laid end to end along the dimension named above; an argument that names none is the same for every part. Nothing has to cross between parts.
Inputs may be any that keep to these rules, and one draw needn't show every extreme that they name: pattern[h, i, 0] = i; only the first counts[h, i] entries of a row are used, and a row may name a block more than once. `counts`: the number of used entries of each row of pattern.
All inputs are finite; a program needn't handle non-finite values.
Results may differ from a plain program's by a relative error of at most 0.012.
Values may be sent and summed in bfloat16 or wider, within the bound.
No kernel may reach another device: no remote copies, remote signals or barrier semaphores. Data moves between devices by JAX's collectives and lax.ppermute only.
A program may use at most 64 MiB of HBM per device.

v0:
```python
import jax
import jax.numpy as jnp
from jax import lax
from jax.sharding import PartitionSpec as P


def as_blocks(tensor, number_blocks):
    return tensor.reshape(number_blocks, -1, tensor.shape[1])


def slot_bound(pattern):
    return pattern.shape[1]


def head_stats(query_head, key_head, pattern, counts):
    number_blocks, slot_count = pattern.shape
    factor = query_head.shape[1] ** (-0.5)
    query_blk = as_blocks(query_head, number_blocks)
    key_blk = as_blocks(key_head, number_blocks)
    key_sets = jnp.take(key_blk, pattern, axis=0)
    scores = (
        jnp.einsum("iqd,ijkd->jiqk", query_blk, key_sets, preferred_element_type=jnp.float32)
        * factor
    )
    active = jnp.arange(slot_count, dtype=jnp.int32)[:, None] < counts[None, :]
    scores = jnp.where(active[:, :, None, None], scores, -jnp.inf)
    row_max = jnp.max(scores, axis=(0, 3))
    row_sum = jnp.sum(jnp.exp(scores - row_max[None, :, :, None]), axis=(0, 3))
    return (row_max, row_sum, scores)


def head_rest(
    query_head, key_head, value_head, grad_head, pattern, counts, row_max, row_sum, scores_all
):
    number_blocks = pattern.shape[0]
    factor = query_head.shape[1] ** (-0.5)
    query_blk = as_blocks(query_head, number_blocks)
    key_blk = as_blocks(key_head, number_blocks)
    value_blk = as_blocks(value_head, number_blocks)
    grad_blk = as_blocks(grad_head, number_blocks)
    bound = slot_bound(pattern)

    def slot_data(position):
        scores = lax.dynamic_index_in_dim(scores_all, position, 0, keepdims=False)
        blocks = lax.dynamic_index_in_dim(pattern, position, 1, keepdims=False)
        probabilities = jnp.exp(scores - row_max[:, :, None]) / row_sum[:, :, None]
        return (probabilities, probabilities.astype(jnp.bfloat16), blocks, position < counts)

    def accumulate(position, attended):
        weights, blocks = slot_data(position)[1:3]
        values = jnp.take(value_blk, blocks, axis=0)
        return attended + jnp.einsum(
            "iqk,ikd->iqd", weights, values, preferred_element_type=jnp.float32
        )

    empty_sum = jnp.zeros(query_blk.shape, jnp.float32)
    attended = lax.fori_loop(0, bound, accumulate, empty_sum)
    row_delta = jnp.sum(grad_blk.astype(jnp.float32) * attended, axis=2)

    def backward(position, running):
        query_sum, key_sum, value_sum = running
        probabilities, weights, blocks, active = slot_data(position)
        gathered = jnp.take(key_blk, blocks, axis=0)
        values = jnp.take(value_blk, blocks, axis=0)
        prob_grad = jnp.einsum("iqd,ikd->iqk", grad_blk, values, preferred_element_type=jnp.float32)
        score_grad = (probabilities * (prob_grad - row_delta[:, :, None])).astype(jnp.bfloat16)
        query_sum = query_sum + jnp.einsum(
            "iqk,ikd->iqd", score_grad, gathered, preferred_element_type=jnp.float32
        )
        key_terms = jnp.einsum(
            "iqk,iqd->ikd", score_grad, query_blk, preferred_element_type=jnp.float32
        )
        value_terms = jnp.einsum(
            "iqk,iqd->ikd", weights, grad_blk, preferred_element_type=jnp.float32
        )
        keep = active[:, None, None]
        key_sum = key_sum.at[blocks].add(jnp.where(keep, key_terms, 0.0))
        value_sum = value_sum.at[blocks].add(jnp.where(keep, value_terms, 0.0))
        return (query_sum, key_sum, value_sum)

    query_sum, key_sum, value_sum = lax.fori_loop(
        0, bound, backward, (empty_sum, empty_sum, empty_sum)
    )
    head_shape = query_head.shape
    return (
        (factor * query_sum).reshape(head_shape).astype(jnp.bfloat16),
        (factor * key_sum).reshape(head_shape).astype(jnp.bfloat16),
        value_sum.reshape(head_shape).astype(jnp.bfloat16),
    )


def shards(query_states, key_states, value_states, out_grad, pattern, counts):
    head_count = pattern.shape[0] * lax.axis_size("seq")
    features = query_states.shape[2] // head_count
    split_shape = (query_states.shape[0], query_states.shape[1], head_count, features)
    query_split = query_states.reshape(split_shape)
    key_split = key_states.reshape(split_shape)
    value_split = value_states.reshape(split_shape)
    grad_split = out_grad.reshape(split_shape)
    stats_map = jax.vmap(jax.vmap(head_stats, in_axes=(1, 1, 0, 0)), in_axes=(0, 0, None, None))
    rest_map = jax.vmap(
        jax.vmap(head_rest, in_axes=(1, 1, 1, 1, 0, 0, 0, 0, 0), out_axes=1),
        in_axes=(0, 0, 0, 0, None, None, 0, 0, 0),
    )
    query_part = lax.all_to_all(query_split, "seq", split_axis=2, concat_axis=1, tiled=True)
    key_part = lax.all_to_all(key_split, "seq", split_axis=2, concat_axis=1, tiled=True)
    value_part = lax.all_to_all(value_split, "seq", split_axis=2, concat_axis=1, tiled=True)
    grad_part = lax.all_to_all(grad_split, "seq", split_axis=2, concat_axis=1, tiled=True)
    row_max, row_sum, scores_all = stats_map(query_part, key_part, pattern, counts)
    gradients = rest_map(
        query_part, key_part, value_part, grad_part, pattern, counts, row_max, row_sum, scores_all
    )
    return (
        lax.all_to_all(gradients[0], "seq", split_axis=1, concat_axis=2, tiled=True).reshape(
            query_states.shape
        ),
        lax.all_to_all(gradients[1], "seq", split_axis=1, concat_axis=2, tiled=True).reshape(
            query_states.shape
        ),
        lax.all_to_all(gradients[2], "seq", split_axis=1, concat_axis=2, tiled=True).reshape(
            query_states.shape
        ),
    )


def solution(mesh):
    placed = (
        P(("groups", "mp", "rep"), "seq", None),
        P(("groups", "mp", "rep"), "seq", None),
        P(("groups", "mp", "rep"), "seq", None),
        P(("groups", "mp", "rep"), "seq", None),
        P("seq", None, None),
        P("seq", None),
    )
    return jax.shard_map(
        shards,
        mesh=mesh,
        in_specs=placed,
        out_specs=(
            P(("groups", "mp", "rep"), "seq", None),
            P(("groups", "mp", "rep"), "seq", None),
            P(("groups", "mp", "rep"), "seq", None),
        ),
        check_vma=False,
    )
```

profile of v0, /device:TPU:0, one launch (start us, length us, event | category | flops | bytes accessed | tf_op | source)
XLA Modules:
  0.0 286.5 jit_solution(13925661281241082270)
XLA Ops:
  3.1 6.3 %all-to-all-start = ((bf16[1,128,16,128]{3,1,0,2:T(8,128)(2,1)}), bf16[1,128,16,128]{3,1,0,2:T(8,128)(2,1)S(1)}, u32[]{:S(2)}, u32[]{:S(2)}) async-start(bf16[1,128,16,128]{3,1,0,2:T(8,128)(2,1)} %copy.88), calls=%async_computation | async-start | bytes 1048576 | tf_op jit(solution)/shard_map/all_to_all | solution.py:106
  11.7 12.2 %all-to-all-done = bf16[1,128,16,128]{3,1,0,2:T(8,128)(2,1)S(1)} async-done(((bf16[1,128,16,128]{3,1,0,2:T(8,128)(2,1)}), bf16[1,128,16,128]{3,1,0,2:T(8,128)(2,1)S(1)}, u32[]{:S(2)}, u32[]{:S(2)}) %all-to-all-start) | async-done | bytes 524320 | tf_op jit(solution)/shard_map/all_to_all | solution.py:106
  23.9 3.5 %all-to-all-start.2 = ((bf16[1,128,16,128]{3,1,0,2:T(8,128)(2,1)}), bf16[1,128,16,128]{3,1,0,2:T(8,128)(2,1)S(1)}, u32[]{:S(2)}, u32[]{:S(2)}) async-start(bf16[1,128,16,128]{3,1,0,2:T(8,128)(2,1)} %copy.94), calls=%async_computation.2 | async-start | bytes 1048576 | tf_op jit(solution)/shard_map/all_to_all | solution.py:107
  28.7 12.7 %all-to-all-done.2 = bf16[1,128,16,128]{3,1,0,2:T(8,128)(2,1)S(1)} async-done(((bf16[1,128,16,128]{3,1,0,2:T(8,128)(2,1)}), bf16[1,128,16,128]{3,1,0,2:T(8,128)(2,1)S(1)}, u32[]{:S(2)}, u32[]{:S(2)}) %all-to-all-start.2) | async-done | bytes 524320 | tf_op jit(solution)/shard_map/all_to_all | solution.py:107
  41.3 3.5 %all-to-all-start.1 = ((bf16[1,128,16,128]{3,1,0,2:T(8,128)(2,1)}), bf16[1,128,16,128]{3,1,0,2:T(8,128)(2,1)S(1)}, u32[]{:S(2)}, u32[]{:S(2)}) async-start(bf16[1,128,16,128]{3,1,0,2:T(8,128)(2,1)} %copy.91), calls=%async_computation.1 | async-start | bytes 1048576 | tf_op jit(solution)/shard_map/all_to_all | solution.py:105
  46.5 3.0 %gather_fusion.3 = bf16[96,128,128]{2,1,0:T(8,128)(2,1)} fusion(bf16[4,4,128,128]{3,2,1,0:T(8,128)(2,1)S(1)} %bitcast.298, s32[96]{0:T(128)S(1)} %reshape.417), kind=kCustom, calls=%fused_computation.3 | custom fusion | bytes 6292224 | tf_op jit(solution)/shard_map/vmap(vmap(jit(_take)))/gather | solution.py:20
  49.6 9.2 %all-to-all-done.1 = bf16[1,128,16,128]{3,1,0,2:T(8,128)(2,1)S(1)} async-done(((bf16[1,128,16,128]{3,1,0,2:T(8,128)(2,1)}), bf16[1,128,16,128]{3,1,0,2:T(8,128)(2,1)S(1)}, u32[]{:S(2)}, u32[]{:S(2)}) %all-to-all-start.1) | async-done | bytes 524320 | tf_op jit(solution)/shard_map/all_to_all | solution.py:105
  58.8 4.1 %all-to-all-start.3 = ((bf16[1,128,16,128]{3,1,0,2:T(8,128)(2,1)}), bf16[1,128,16,128]{3,1,0,2:T(8,128)(2,1)}, u32[]{:S(2)}, u32[]{:S(2)}) async-start(bf16[1,128,16,128]{3,1,0,2:T(8,128)(2,1)} %copy.97), calls=%async_computation.3 | async-start | bytes 1048576 | tf_op jit(solution)/shard_map/all_to_all | solution.py:108
  62.9 2.7 fusion.48
  66.6 1.8 copy-done.3
  68.3 49.0 %while.36 = (s32[]{:T(128)}, f32[1,4,4,128,128]{4,3,2,1,0:T(8,128)}, f32[1,4,6,4,128,128]{4,5,2,3,1,0:T(8,128)}, f32[1,4,4,128]{3,2,1,0:T(4,128)S(1)}, f32[1,4,4...) while((s32[]{:T(128)}, ...), condition=%wide.region_3.5_spmd.clone, body=%wide.region_2.4_spmd.clone.sunk | while | flops 68681968 | bytes 8929951 | solution.py:57
  73.4 2.9 %fusion.67 = f32[1,4,4,128,128]{4,3,2,1,0:T(8,128)} fusion(f32[1,4,4,128,128]{4,3,2,1,0:T(8,128)} %get-tuple-element.813, f32[1,4,1,4,128,128]{5,4,3,1,2,0:T(8,128)S(1)} %copy.137, bf16[1,4,4,128,128]{4,3,2,1,0:T(8,128)(2,1)} %bitcast.310, f32[4,4,128]{2,1,0:T(4,128)S(1)} %bitcast.335, f32[4,4,128]{2,1,0:T(4,128)S(1)} %bitcast.331, ...), kind=kOutput, calls=%fused_computation.7.clone.1 | convolution fusion | flops 68681728 | bytes 3686417 | tf_op jit(solution)/shard_map/vmap(vmap())/while/body/eval_jaxpr/iqk,ikd->iqd/dot_general | solution.py:52
  81.5 3.1 %fusion.67 = f32[1,4,4,128,128]{4,3,2,1,0:T(8,128)} fusion(f32[1,4,4,128,128]{4,3,2,1,0:T(8,128)} %get-tuple-element.813, f32[1,4,1,4,128,128]{5,4,3,1,2,0:T(8,128)S(1)} %copy.137, bf16[1,4,4,128,128]{4,3,2,1,0:T(8,128)(2,1)} %bitcast.310, f32[4,4,128]{2,1,0:T(4,128)S(1)} %bitcast.335, f32[4,4,128]{2,1,0:T(4,128)S(1)} %bitcast.331, ...), kind=kOutput, calls=%fused_computation.7.clone.1 | convolution fusion | flops 68681728 | bytes 3686417 | tf_op jit(solution)/shard_map/vmap(vmap())/while/body/eval_jaxpr/iqk,ikd->iqd/dot_general | solution.py:52
  89.7 3.1 %fusion.67 = f32[1,4,4,128,128]{4,3,2,1,0:T(8,128)} fusion(f32[1,4,4,128,128]{4,3,2,1,0:T(8,128)} %get-tuple-element.813, f32[1,4,1,4,128,128]{5,4,3,1,2,0:T(8,128)S(1)} %copy.137, bf16[1,4,4,128,128]{4,3,2,1,0:T(8,128)(2,1)} %bitcast.310, f32[4,4,128]{2,1,0:T(4,128)S(1)} %bitcast.335, f32[4,4,128]{2,1,0:T(4,128)S(1)} %bitcast.331, ...), kind=kOutput, calls=%fused_computation.7.clone.1 | convolution fusion | flops 68681728 | bytes 3686417 | tf_op jit(solution)/shard_map/vmap(vmap())/while/body/eval_jaxpr/iqk,ikd->iqd/dot_general | solution.py:52
  97.9 3.1 %fusion.67 = f32[1,4,4,128,128]{4,3,2,1,0:T(8,128)} fusion(f32[1,4,4,128,128]{4,3,2,1,0:T(8,128)} %get-tuple-element.813, f32[1,4,1,4,128,128]{5,4,3,1,2,0:T(8,128)S(1)} %copy.137, bf16[1,4,4,128,128]{4,3,2,1,0:T(8,128)(2,1)} %bitcast.310, f32[4,4,128]{2,1,0:T(4,128)S(1)} %bitcast.335, f32[4,4,128]{2,1,0:T(4,128)S(1)} %bitcast.331, ...), kind=kOutput, calls=%fused_computation.7.clone.1 | convolution fusion | flops 68681728 | bytes 3686417 | tf_op jit(solution)/shard_map/vmap(vmap())/while/body/eval_jaxpr/iqk,ikd->iqd/dot_general | solution.py:52
  106.1 3.1 %fusion.67 = f32[1,4,4,128,128]{4,3,2,1,0:T(8,128)} fusion(f32[1,4,4,128,128]{4,3,2,1,0:T(8,128)} %get-tuple-element.813, f32[1,4,1,4,128,128]{5,4,3,1,2,0:T(8,128)S(1)} %copy.137, bf16[1,4,4,128,128]{4,3,2,1,0:T(8,128)(2,1)} %bitcast.310, f32[4,4,128]{2,1,0:T(4,128)S(1)} %bitcast.335, f32[4,4,128]{2,1,0:T(4,128)S(1)} %bitcast.331, ...), kind=kOutput, calls=%fused_computation.7.clone.1 | convolution fusion | flops 68681728 | bytes 3686417 | tf_op jit(solution)/shard_map/vmap(vmap())/while/body/eval_jaxpr/iqk,ikd->iqd/dot_general | solution.py:52
  114.3 3.1 %fusion.67 = f32[1,4,4,128,128]{4,3,2,1,0:T(8,128)} fusion(f32[1,4,4,128,128]{4,3,2,1,0:T(8,128)} %get-tuple-element.813, f32[1,4,1,4,128,128]{5,4,3,1,2,0:T(8,128)S(1)} %copy.137, bf16[1,4,4,128,128]{4,3,2,1,0:T(8,128)(2,1)} %bitcast.310, f32[4,4,128]{2,1,0:T(4,128)S(1)} %bitcast.335, f32[4,4,128]{2,1,0:T(4,128)S(1)} %bitcast.331, ...), kind=kOutput, calls=%fused_computation.7.clone.1 | convolution fusion | flops 68681728 | bytes 3686417 | tf_op jit(solution)/shard_map/vmap(vmap())/while/body/eval_jaxpr/iqk,ikd->iqd/dot_general | solution.py:52
  117.4 1.9 copy.134
  119.2 1.9 copy.132
  125.1 103.7 %while.37 = (s32[]{:T(128)}, f32[1,4,4,128,128]{4,3,2,1,0:T(8,128)}, f32[1,4,4,128,128]{4,3,2,1,0:T(8,128)}, f32[1,4,4,128,128]{4,3,2,1,0:T(8,128)}, f32[1,4,6,4...) while((s32[]{:T(128)}, ...), condition=%wide.region_8.10_spmd.clone, body=%wide.region_5.9_spmd.clone.sunk | while | flops 272630176 | bytes 27305432 | solution.py:81
  128.0 2.0 fusion.77
  131.4 3.5 %scatter_fusion = f32[4,4,128,128]{3,2,1,0:T(8,128)} fusion(f32[4,4,128,128]{3,2,1,0:T(8,128)} %bitcast.305, s32[16]{0:T(128)S(1)} %reshape.541, f32[16,128,128]{2,1,0:T(8,128)S(1)} %bitcast.297), kind=kCustom, calls=%fused_computation.4.clone.clone.1 | custom fusion | flops 262144 | bytes 3145856 | tf_op jit(solution)/shard_map/vmap(vmap())/while/body/eval_jaxpr/scatter-add | solution.py:77
  138.7 1.7 scatter_fusion.1
  144.3 2.0 fusion.77
  147.7 3.5 %scatter_fusion = f32[4,4,128,128]{3,2,1,0:T(8,128)} fusion(f32[4,4,128,128]{3,2,1,0:T(8,128)} %bitcast.305, s32[16]{0:T(128)S(1)} %reshape.541, f32[16,128,128]{2,1,0:T(8,128)S(1)} %bitcast.297), kind=kCustom, calls=%fused_computation.4.clone.clone.1 | custom fusion | flops 262144 | bytes 3145856 | tf_op jit(solution)/shard_map/vmap(vmap())/while/body/eval_jaxpr/scatter-add | solution.py:77
  151.8 2.6 fusion.78
  161.8 2.0 fusion.77
  165.2 3.5 %scatter_fusion = f32[4,4,128,128]{3,2,1,0:T(8,128)} fusion(f32[4,4,128,128]{3,2,1,0:T(8,128)} %bitcast.305, s32[16]{0:T(128)S(1)} %reshape.541, f32[16,128,128]{2,1,0:T(8,128)S(1)} %bitcast.297), kind=kCustom, calls=%fused_computation.4.clone.clone.1 | custom fusion | flops 262144 | bytes 3145856 | tf_op jit(solution)/shard_map/vmap(vmap())/while/body/eval_jaxpr/scatter-add | solution.py:77
  169.3 2.6 fusion.78
  173.6 1.7 scatter_fusion.1
  179.3 2.0 fusion.77
  182.7 3.4 %scatter_fusion = f32[4,4,128,128]{3,2,1,0:T(8,128)} fusion(f32[4,4,128,128]{3,2,1,0:T(8,128)} %bitcast.305, s32[16]{0:T(128)S(1)} %reshape.541, f32[16,128,128]{2,1,0:T(8,128)S(1)} %bitcast.297), kind=kCustom, calls=%fused_computation.4.clone.clone.1 | custom fusion | flops 262144 | bytes 3145856 | tf_op jit(solution)/shard_map/vmap(vmap())/while/body/eval_jaxpr/scatter-add | solution.py:77
  186.7 2.6 fusion.78
  196.7 2.0 fusion.77
  200.1 3.5 %scatter_fusion = f32[4,4,128,128]{3,2,1,0:T(8,128)} fusion(f32[4,4,128,128]{3,2,1,0:T(8,128)} %bitcast.305, s32[16]{0:T(128)S(1)} %reshape.541, f32[16,128,128]{2,1,0:T(8,128)S(1)} %bitcast.297), kind=kCustom, calls=%fused_computation.4.clone.clone.1 | custom fusion | flops 262144 | bytes 3145856 | tf_op jit(solution)/shard_map/vmap(vmap())/while/body/eval_jaxpr/scatter-add | solution.py:77
  204.2 2.6 fusion.78
  208.6 1.7 scatter_fusion.1
  214.2 2.0 fusion.77
  217.6 3.5 %scatter_fusion = f32[4,4,128,128]{3,2,1,0:T(8,128)} fusion(f32[4,4,128,128]{3,2,1,0:T(8,128)} %bitcast.305, s32[16]{0:T(128)S(1)} %reshape.541, f32[16,128,128]{2,1,0:T(8,128)S(1)} %bitcast.297), kind=kCustom, calls=%fused_computation.4.clone.clone.1 | custom fusion | flops 262144 | bytes 3145856 | tf_op jit(solution)/shard_map/vmap(vmap())/while/body/eval_jaxpr/scatter-add | solution.py:77
  221.7 2.6 fusion.78
  226.1 1.7 scatter_fusion.1
  228.9 1.9 multiply_convert_fusion
  231.9 5.0 %all-to-all-start.4 = ((bf16[1,512,4,128]{3,2,0,1:T(4,128)(2,1)}), bf16[1,512,4,128]{3,2,0,1:T(4,128)(2,1)S(1)}, u32[]{:S(2)}, u32[]{:S(2)}) async-start(bf16[1,512,4,128]{3,2,0,1:T(4,128)(2,1)} %bitcast.42), calls=%async_computation.4 | async-start | bytes 1048576 | tf_op jit(solution)/shard_map/all_to_all | solution.py:114
  238.2 12.2 %all-to-all-done.4 = bf16[1,512,4,128]{3,2,0,1:T(4,128)(2,1)S(1)} async-done(((bf16[1,512,4,128]{3,2,0,1:T(4,128)(2,1)}), bf16[1,512,4,128]{3,2,0,1:T(4,128)(2,1)S(1)}, u32[]{:S(2)}, u32[]{:S(2)}) %all-to-all-start.4) | async-done | bytes 524320 | tf_op jit(solution)/shard_map/all_to_all | solution.py:114
  250.4 3.5 %all-to-all-start.5 = ((bf16[1,512,4,128]{3,2,0,1:T(4,128)(2,1)}), bf16[1,512,4,128]{3,2,0,1:T(4,128)(2,1)S(1)}, u32[]{:S(2)}, u32[]{:S(2)}) async-start(bf16[1,512,4,128]{3,2,0,1:T(4,128)(2,1)} %bitcast.47), calls=%async_computation.5 | async-start | bytes 1048576 | tf_op jit(solution)/shard_map/all_to_all | solution.py:117
  255.2 12.6 %all-to-all-done.5 = bf16[1,512,4,128]{3,2,0,1:T(4,128)(2,1)S(1)} async-done(((bf16[1,512,4,128]{3,2,0,1:T(4,128)(2,1)}), bf16[1,512,4,128]{3,2,0,1:T(4,128)(2,1)S(1)}, u32[]{:S(2)}, u32[]{:S(2)}) %all-to-all-start.5) | async-done | bytes 524320 | tf_op jit(solution)/shard_map/all_to_all | solution.py:117
  267.7 3.5 %all-to-all-start.6 = ((bf16[1,512,4,128]{3,2,0,1:T(4,128)(2,1)}), bf16[1,512,4,128]{3,2,0,1:T(4,128)(2,1)S(1)}, u32[]{:S(2)}, u32[]{:S(2)}) async-start(bf16[1,512,4,128]{3,2,0,1:T(4,128)(2,1)} %bitcast.52), calls=%async_computation.6 | async-start | bytes 1048576 | tf_op jit(solution)/shard_map/all_to_all | solution.py:120
  274.0 11.2 %all-to-all-done.6 = bf16[1,512,4,128]{3,2,0,1:T(4,128)(2,1)S(1)} async-done(((bf16[1,512,4,128]{3,2,0,1:T(4,128)(2,1)}), bf16[1,512,4,128]{3,2,0,1:T(4,128)(2,1)S(1)}, u32[]{:S(2)}, u32[]{:S(2)}) %all-to-all-start.6) | async-done | bytes 524320 | tf_op jit(solution)/shard_map/all_to_all | solution.py:120
  (207 shorter events, 101.4 us)
Async XLA Ops:
  0.6 26.7 %copy-start.5 = (bf16[1,128,2048]{2,1,0:T(8,128)(2,1)S(1)}, bf16[1,128,2048]{2,1,0:T(8,128)(2,1)}, u32[]{:S(2)}) copy-start(bf16[1,128,2048]{2,1,0:T(8,128)(2,1)} %param.12) | copy-start | bytes 1572868
  0.6 44.2 %copy-start.8 = (s32[4,4,6]{2,1,0:T(4,128)S(1)}, s32[4,4,6]{2,1,0:T(4,128)}, u32[]{:S(2)}) copy-start(s32[4,4,6]{2,1,0:T(4,128)} %param.16) | copy-start | bytes 1156
  0.7 44.4 %copy-start.6 = (bf16[1,128,2048]{2,1,0:T(8,128)(2,1)S(1)}, bf16[1,128,2048]{2,1,0:T(8,128)(2,1)}, u32[]{:S(2)}) copy-start(bf16[1,128,2048]{2,1,0:T(8,128)(2,1)} %param.15) | copy-start | bytes 1572868
  0.7 45.7 %copy-start.7 = (s32[4,4]{1,0:T(4,128)S(1)}, s32[4,4]{1,0:T(4,128)}, u32[]{:S(2)}) copy-start(s32[4,4]{1,0:T(4,128)} %param.17) | copy-start | bytes 196
  3.1 20.8 %all-to-all-start = ((bf16[1,128,16,128]{3,1,0,2:T(8,128)(2,1)}), bf16[1,128,16,128]{3,1,0,2:T(8,128)(2,1)S(1)}, u32[]{:S(2)}, u32[]{:S(2)}) async-start(bf16[1,128,16,128]{3,1,0,2:T(8,128)(2,1)} %copy.88), calls=%async_computation | async-start | bytes 1048576 | tf_op jit(solution)/shard_map/all_to_all | solution.py:106
  23.9 17.4 %all-to-all-start.2 = ((bf16[1,128,16,128]{3,1,0,2:T(8,128)(2,1)}), bf16[1,128,16,128]{3,1,0,2:T(8,128)(2,1)S(1)}, u32[]{:S(2)}, u32[]{:S(2)}) async-start(bf16[1,128,16,128]{3,1,0,2:T(8,128)(2,1)} %copy.94), calls=%async_computation.2 | async-start | bytes 1048576 | tf_op jit(solution)/shard_map/all_to_all | solution.py:107
  41.3 17.4 %all-to-all-start.1 = ((bf16[1,128,16,128]{3,1,0,2:T(8,128)(2,1)}), bf16[1,128,16,128]{3,1,0,2:T(8,128)(2,1)S(1)}, u32[]{:S(2)}, u32[]{:S(2)}) async-start(bf16[1,128,16,128]{3,1,0,2:T(8,128)(2,1)} %copy.91), calls=%async_computation.1 | async-start | bytes 1048576 | tf_op jit(solution)/shard_map/all_to_all | solution.py:105
  58.8 6.9 %copy-start.4 = (bf16[1,128,16,128]{3,1,0,2:T(8,128)(2,1)}, bf16[1,128,16,128]{3,1,0,2:T(8,128)(2,1)S(1)}, u32[]{:S(2)}) copy-start(bf16[1,128,16,128]{3,1,0,2:T(8,128)(2,1)S(1)} %all-to-all-done.1) | copy-start | bytes 1572868
  58.8 60.5 %all-to-all-start.3 = ((bf16[1,128,16,128]{3,1,0,2:T(8,128)(2,1)}), bf16[1,128,16,128]{3,1,0,2:T(8,128)(2,1)}, u32[]{:S(2)}, u32[]{:S(2)}) async-start(bf16[1,128,16,128]{3,1,0,2:T(8,128)(2,1)} %copy.97), calls=%async_computation.3 | async-start | bytes 1048576 | tf_op jit(solution)/shard_map/all_to_all | solution.py:108
  65.7 2.6 copy-start.3
  134.9 3.8 %copy-start = (f32[1,4,4,128,128]{4,3,2,1,0:T(8,128)S(1)}, f32[1,4,4,128,128]{4,3,2,1,0:T(8,128)}, u32[]{:S(2)}) copy-start(f32[1,4,4,128,128]{4,3,2,1,0:T(8,128)} %get-tuple-element.852) | copy-start | bytes 3145732 | tf_op jit(solution)/shard_map/vmap(vmap())/while
  140.4 1.1 copy-start.1
  151.2 5.0 %copy-start = (f32[1,4,4,128,128]{4,3,2,1,0:T(8,128)S(1)}, f32[1,4,4,128,128]{4,3,2,1,0:T(8,128)}, u32[]{:S(2)}) copy-start(f32[1,4,4,128,128]{4,3,2,1,0:T(8,128)} %get-tuple-element.852) | copy-start | bytes 3145732 | tf_op jit(solution)/shard_map/vmap(vmap())/while
  157.9 1.1 copy-start.1
  168.6 5.0 %copy-start = (f32[1,4,4,128,128]{4,3,2,1,0:T(8,128)S(1)}, f32[1,4,4,128,128]{4,3,2,1,0:T(8,128)}, u32[]{:S(2)}) copy-start(f32[1,4,4,128,128]{4,3,2,1,0:T(8,128)} %get-tuple-element.852) | copy-start | bytes 3145732 | tf_op jit(solution)/shard_map/vmap(vmap())/while
  175.4 1.1 copy-start.1
  186.1 5.0 %copy-start = (f32[1,4,4,128,128]{4,3,2,1,0:T(8,128)S(1)}, f32[1,4,4,128,128]{4,3,2,1,0:T(8,128)}, u32[]{:S(2)}) copy-start(f32[1,4,4,128,128]{4,3,2,1,0:T(8,128)} %get-tuple-element.852) | copy-start | bytes 3145732 | tf_op jit(solution)/shard_map/vmap(vmap())/while
  192.8 1.1 copy-start.1
  203.6 5.0 %copy-start = (f32[1,4,4,128,128]{4,3,2,1,0:T(8,128)S(1)}, f32[1,4,4,128,128]{4,3,2,1,0:T(8,128)}, u32[]{:S(2)}) copy-start(f32[1,4,4,128,128]{4,3,2,1,0:T(8,128)} %get-tuple-element.852) | copy-start | bytes 3145732 | tf_op jit(solution)/shard_map/vmap(vmap())/while
  210.3 1.1 copy-start.1
  221.1 5.0 %copy-start = (f32[1,4,4,128,128]{4,3,2,1,0:T(8,128)S(1)}, f32[1,4,4,128,128]{4,3,2,1,0:T(8,128)}, u32[]{:S(2)}) copy-start(f32[1,4,4,128,128]{4,3,2,1,0:T(8,128)} %get-tuple-element.852) | copy-start | bytes 3145732 | tf_op jit(solution)/shard_map/vmap(vmap())/while
  227.8 1.1 copy-start.1
  228.9 25.0 %copy-start.2 = (f32[1,4,4,128,128]{4,3,2,1,0:T(8,128)S(1)}, f32[1,4,4,128,128]{4,3,2,1,0:T(8,128)}, u32[]{:S(2)}) copy-start(f32[1,4,4,128,128]{4,3,2,1,0:T(8,128)} %get-tuple-element.362) | copy-start | bytes 3145732
  231.9 18.4 %all-to-all-start.4 = ((bf16[1,512,4,128]{3,2,0,1:T(4,128)(2,1)}), bf16[1,512,4,128]{3,2,0,1:T(4,128)(2,1)S(1)}, u32[]{:S(2)}, u32[]{:S(2)}) async-start(bf16[1,512,4,128]{3,2,0,1:T(4,128)(2,1)} %bitcast.42), calls=%async_computation.4 | async-start | bytes 1048576 | tf_op jit(solution)/shard_map/all_to_all | solution.py:114
  250.4 17.3 %all-to-all-start.5 = ((bf16[1,512,4,128]{3,2,0,1:T(4,128)(2,1)}), bf16[1,512,4,128]{3,2,0,1:T(4,128)(2,1)S(1)}, u32[]{:S(2)}, u32[]{:S(2)}) async-start(bf16[1,512,4,128]{3,2,0,1:T(4,128)(2,1)} %bitcast.47), calls=%async_computation.5 | async-start | bytes 1048576 | tf_op jit(solution)/shard_map/all_to_all | solution.py:117
  267.7 17.4 %all-to-all-start.6 = ((bf16[1,512,4,128]{3,2,0,1:T(4,128)(2,1)}), bf16[1,512,4,128]{3,2,0,1:T(4,128)(2,1)S(1)}, u32[]{:S(2)}, u32[]{:S(2)}) async-start(bf16[1,512,4,128]{3,2,0,1:T(4,128)(2,1)} %bitcast.52), calls=%async_computation.6 | async-start | bytes 1048576 | tf_op jit(solution)/shard_map/all_to_all | solution.py:120
where the time goes:
time: 289 us; the launch traced here: 287 us
  waiting for transfers between devices  70 us (24%)
  local copies, waits for them, and re-layouts  67.4 us (23%)
  matrix products  65.7 us (23%)
  other arithmetic  52.5 us (18%)
  starting transfers between devices  29.4 us (10%)
    scatter-add x12, other arithmetic, backward(): key_sum = key_sum.at[blocks].add(jnp.where(keep, key_terms, 0.0))  24.8 us
    dot_general x6, matrix products, accumulate(): jnp.einsum('iqk,ikd->iqd', weights, values, preferred_element_type=jnp.fl...  18.3 us
    dot_general x6, matrix products, backward(): jnp.einsum('iqk,ikd->iqd', score_grad, gathered, preferred_element_type=j...  14.5 us
    all_to_all x1, waiting for transfers between devices, shards(): lax.all_to_all(value_split, 'seq', split_axis=2, concat_axis=1, tiled=True)  12.7 us
    all_to_all x1, waiting for transfers between devices, shards(): lax.all_to_all(gradients[1], 'seq', split_axis=1, concat_axis=2, tiled=True)  12.6 us
    all_to_all x1, waiting for transfers between devices, shards(): lax.all_to_all(gradients[0], 'seq', split_axis=1, concat_axis=2, tiled=True)  12.2 us
    all_to_all x1, waiting for transfers between devices, shards(): lax.all_to_all(key_split, 'seq', split_axis=2, concat_axis=1, tiled=True)  12.2 us
    dot_general x6, matrix products, backward(): jnp.einsum('iqd,ikd->iqk', grad_blk, values, preferred_element_type=jnp.f...  11.8 us
  transfers between devices with their start and end apart: 7, of which 6 were waited for; matrix products, arithmetic and copies ran while one was open for 24% of the time, Pallas kernels for 0%

commit v1 on v0

v1 whole, which is shorter than its diff:
```python
import functools
import math

import jax
import jax.numpy as jnp
from jax import lax
from jax.experimental import pallas as pl
from jax.experimental.pallas import tpu as pltpu
from jax.sharding import PartitionSpec as P

LOG2E = math.log2(math.e)
NT = (((1,), (1,)), ((), ()))
NN = (((1,), (0,)), ((), ()))
VMEM_LIMIT = 48 * 1024 * 1024


def dot(left, right, dims=NN):
    return lax.dot_general(left, right, dims, preferred_element_type=jnp.float32)


def pack_kernel(size, width, offset, place, *refs):
    sources, outs, (held, in_sems, out_sems) = refs[:4], refs[4:-3], refs[-3:]
    position = place[0]
    total = sources[0].shape[2]
    reads, writes = [], []
    for step in range(1, size):
        start = lax.rem(position + step, size) * (total // size) + offset
        columns = pl.ds(pl.multiple_of(start, 128), width)
        reads.append(
            [
                pltpu.make_async_copy(
                    source.at[0, :, columns], held.at[step - 1, index], in_sems.at[step - 1, index]
                )
                for index, source in enumerate(sources)
            ]
        )
        writes.append(pltpu.make_async_copy(held.at[step - 1], outs[step - 1], out_sems.at[step - 1]))
    for read in sum(reads, []):
        read.start()
    for read, write in zip(reads, writes):
        for one in read:
            one.wait()
        write.start()
    for write in writes:
        write.wait()


def pack(size, width, offset, place, sources):
    tokens = sources[0].shape[1]
    return pl.pallas_call(
        functools.partial(pack_kernel, size, width, offset),
        out_shape=[jax.ShapeDtypeStruct((4, tokens, width), jnp.bfloat16)] * (size - 1),
        in_specs=[pl.BlockSpec(memory_space=pltpu.SMEM)] + [pl.BlockSpec(memory_space=pl.ANY)] * 4,
        out_specs=[pl.BlockSpec(memory_space=pl.ANY)] * (size - 1),
        scratch_shapes=[
            pltpu.VMEM((size - 1, 4, tokens, width), jnp.bfloat16),
            pltpu.SemaphoreType.DMA((size - 1, 4)),
            pltpu.SemaphoreType.DMA((size - 1,)),
        ],
        compiler_params=pltpu.CompilerParams(vmem_limit_bytes=VMEM_LIMIT),
        name="pack",
    )(place, *sources)


def heads_kernel(size, heads, first, block, place, uses, *refs):
    own_refs, far_refs = refs[:4], refs[4 : 3 + size]
    out_refs = refs[3 + size : 3 + 2 * size]
    joined, key_flip, key_sum, value_sum = refs[3 + 2 * size :]
    position = place[0]
    tokens, features = own_refs[0].shape[1], joined.shape[2]
    length = size * tokens
    blocks = length // block
    local = tokens // block
    chunk = min(length, max(2 * block, 256))
    factor = features**-0.5

    def origin(index):
        return lax.rem(position + size - index // local, size) * local + index % local

    def one_chunk(head, number):
        start = pl.multiple_of(number * chunk, chunk)
        rows = pl.ds(start, chunk)
        query, grad = joined[0, rows, :], joined[3, rows, :]
        scores = dot(joined[1], query, NT)
        prob_grad = dot(joined[2], grad, NT)
        weight_parts, score_parts = [], []
        for part in range(chunk // block):
            row = origin(number * (chunk // block) + part)
            columns = slice(part * block, (part + 1) * block)
            counts = [uses[first + head, row, origin(j)] for j in range(blocks)]
            terms = []
            for j in range(blocks):
                term = scores[j * block : (j + 1) * block, columns] * (factor * LOG2E)
                terms.append(term + jnp.where(counts[j] > 0, 0.0, -jnp.inf))
            top = functools.reduce(jnp.maximum, terms)
            top = jnp.max(top, axis=0, keepdims=True)
            exps = [jnp.exp2(term - top) for term in terms]
            grads = [prob_grad[j * block : (j + 1) * block, columns] for j in range(blocks)]
            total = sum(count * e for count, e in zip(counts, exps))
            moment = sum(count * (e * g) for count, e, g in zip(counts, exps, grads))
            inverse = 1.0 / jnp.sum(total, axis=0, keepdims=True)
            delta = jnp.sum(moment, axis=0, keepdims=True) * inverse
            probs = [e * (inverse * count) for count, e in zip(counts, exps)]
            weight_parts.append(jnp.concatenate([p.astype(jnp.bfloat16) for p in probs], axis=0))
            score_parts.append(
                jnp.concatenate(
                    [(p * (g - delta)).astype(jnp.bfloat16) for p, g in zip(probs, grads)], axis=0
                )
            )
        weights = jnp.concatenate(weight_parts, axis=1)
        score_grad = jnp.concatenate(score_parts, axis=1)
        key_sum[...] += dot(score_grad, query)
        value_sum[...] += dot(weights, grad)
        flipped = dot(key_flip[...], score_grad)
        return (flipped.T * factor).astype(jnp.bfloat16)

    for head in range(heads):
        features_at = pl.ds(head * features, features)
        for index in range(4):
            joined[index, pl.ds(0, tokens), :] = own_refs[index][0, :, features_at]
            for step in range(1, size):
                joined[index, pl.ds(step * tokens, tokens), :] = far_refs[step - 1][index, :, features_at]
        key_flip[...] = joined[1].T
        key_sum[...] = jnp.zeros_like(key_sum)
        value_sum[...] = jnp.zeros_like(value_sum)

        for number in range(length // chunk):
            query_grad = one_chunk(head, number)
            for part in range(max(1, chunk // tokens)):
                step, within = divmod(number * chunk + part * tokens, tokens)
                span = min(chunk, tokens)
                out_refs[step][0, pl.ds(within, span), features_at] = query_grad[part * span : (part + 1) * span]
        for step in range(size):
            rows = pl.ds(step * tokens, tokens)
            out_refs[step][1, :, features_at] = (factor * key_sum[rows, :]).astype(jnp.bfloat16)
            out_refs[step][2, :, features_at] = value_sum[rows, :].astype(jnp.bfloat16)


def run_heads(size, heads, first, block, place, uses, owns, fars):
    tokens = owns[0].shape[1]
    features = fars[0].shape[2] // heads
    width = heads * features
    length = size * tokens
    per_device = owns[0].shape[2] // size // width

    def own_map(place):
        return (0, 0, place[0] * per_device + first // heads)

    own_spec = pl.BlockSpec((1, tokens, width), lambda i, place: own_map(place))
    far_spec = pl.BlockSpec((4, tokens, width), lambda i, place: (0, 0, 0))
    out_spec = pl.BlockSpec((3, tokens, width), lambda i, place: (0, 0, 0))
    return pl.pallas_call(
        functools.partial(heads_kernel, size, heads, first, block),
        grid_spec=pltpu.PrefetchScalarGridSpec(
            num_scalar_prefetch=1,
            grid=(1,),
            in_specs=[pl.BlockSpec(memory_space=pltpu.SMEM)] + [own_spec] * 4 + [far_spec] * (size - 1),
            out_specs=[out_spec] * size,
            scratch_shapes=[
                pltpu.VMEM((4, length, features), jnp.bfloat16),
                pltpu.VMEM((features, length), jnp.bfloat16),
                pltpu.VMEM((length, features), jnp.float32),
                pltpu.VMEM((length, features), jnp.float32),
            ],
        ),
        out_shape=[jax.ShapeDtypeStruct((3, tokens, width), jnp.bfloat16)] * size,
        compiler_params=pltpu.CompilerParams(vmem_limit_bytes=VMEM_LIMIT),
        cost_estimate=pl.CostEstimate(
            flops=heads * 10 * length * length * features,
            bytes_accessed=heads * 14 * length * features,
            transcendentals=heads * length * length,
        ),
        name="heads",
    )(place, uses, *owns, *fars)


def place_kernel(size, groups, width, place, *refs):
    parts, outs = refs[: size * groups], refs[size * groups : -3]
    held, in_sems, out_sems = refs[-3:]
    position = place[0]
    total = outs[0].shape[2]
    reads, writes = [], []
    for step in range(size):
        start = pl.multiple_of(lax.rem(position + step, size) * (total // size), 128)
        reads.append(
            [
                pltpu.make_async_copy(
                    parts[group * size + step],
                    held.at[step, :, :, pl.ds(group * width, width)],
                    in_sems.at[step, group],
                )
                for group in range(groups)
            ]
        )
        writes.append(
            [
                pltpu.make_async_copy(
                    held.at[step, index],
                    out.at[0, :, pl.ds(start, total // size)],
                    out_sems.at[step, index],
                )
                for index, out in enumerate(outs)
            ]
        )
    for read in sum(reads, []):
        read.start()
    for read, write in zip(reads, writes):
        for one in read:
            one.wait()
        for one in write:
            one.start()
    for one in sum(writes, []):
        one.wait()


def put_in_place(size, groups, width, place, parts, shape):
    return pl.pallas_call(
        functools.partial(place_kernel, size, groups, width),
        out_shape=[jax.ShapeDtypeStruct(shape, jnp.bfloat16)] * 3,
        in_specs=[pl.BlockSpec(memory_space=pltpu.SMEM)] + [pl.BlockSpec(memory_space=pl.ANY)] * len(parts),
        out_specs=[pl.BlockSpec(memory_space=pl.ANY)] * 3,
        scratch_shapes=[
            pltpu.VMEM((size, 3, shape[1], groups * width), jnp.bfloat16),
            pltpu.SemaphoreType.DMA((size, groups)),
            pltpu.SemaphoreType.DMA((size, 3)),
        ],
        compiler_params=pltpu.CompilerParams(vmem_limit_bytes=VMEM_LIMIT),
        name="put_in_place",
    )(place, *parts)


def shards(query_states, key_states, value_states, out_grad, pattern, counts):
    size = lax.axis_size("seq")
    place = lax.axis_index("seq").astype(jnp.int32).reshape(1)
    local_heads, blocks, slots = pattern.shape
    tokens, total = query_states.shape[1:]
    features = total // (local_heads * size)
    block = tokens * size // blocks
    sources = (query_states, key_states, value_states, out_grad)

    used = jnp.arange(slots, dtype=jnp.int32) < counts[:, :, None]
    named = pattern[..., None] == jnp.arange(blocks, dtype=jnp.int32)
    uses = jnp.sum(jnp.where(used[..., None] & named, 1.0, 0.0), axis=2, dtype=jnp.float32)

    heads = 2 if local_heads % 2 == 0 else 1
    groups = local_heads // heads
    width = heads * features
    parts = []
    for group in range(groups):
        packed = pack(size, width, group * width, place, sources)
        fars = [
            lax.ppermute(packed[s - 1], "seq", [(j, (j + s) % size) for j in range(size)])
            for s in range(1, size)
        ]
        outs = run_heads(size, heads, group * heads, block, place, uses, sources, fars)
        parts.append(outs[0])
        parts += [
            lax.ppermute(outs[s], "seq", [(j, (j - s) % size) for j in range(size)])
            for s in range(1, size)
        ]
    return tuple(put_in_place(size, groups, width, place, parts, query_states.shape))


def solution(mesh):
    tokens = P(("groups", "mp", "rep"), "seq", None)
    return jax.shard_map(
        shards,
        mesh=mesh,
        in_specs=(tokens, tokens, tokens, tokens, P("seq", None, None), P("seq", None)),
        out_specs=(tokens, tokens, tokens),
        check_vma=False,
    )
```

time: 289 us -> 91.5 us (0.32)
  matrix products: 65.7 us -> 0 us
  local copies, waits for them, and re-layouts: 67.4 us -> 4.17 us
  other arithmetic: 52.5 us -> 0.18 us
  waiting for transfers between devices: 70 us -> 31.2 us
  starting transfers between devices: 29.4 us -> 46.3 us
  Pallas kernels: 0 us -> 8.65 us
    all_to_all x7 -> x0, waiting for transfers between devices: 70 us -> none  [the longest x1 12.7 us: shards(): lax.all_to_all(value_split, 'seq', split_axis=2, concat_axis=1, tiled=True)]
    dot_general x31 -> x0, matrix products: 65.7 us -> none  [the longest x6 18.3 us: accumulate(): jnp.einsum('iqk,ikd->iqd', weights, values, preferred_element_type=jnp.fl...]
    ppermute x0 -> x12, starting transfers between devices: none -> 46.3 us  [the longest x6 35.7 us: shards(): lax.ppermute(outs[s], 'seq', [(j, (j - s) % size) for j in range(size)])]
    scatter-add x18 -> x0, other arithmetic: 35.1 us -> none  [the longest x12 24.8 us: backward(): key_sum = key_sum.at[blocks].add(jnp.where(keep, key_terms, 0.0))]
    ppermute x0 -> x12, waiting for transfers between devices: none -> 31.2 us  [the longest x6 18.6 us: shards(): lax.ppermute(outs[s], 'seq', [(j, (j - s) % size) for j in range(size)])]
    all_to_all x7 -> x0, starting transfers between devices: 29.4 us -> none  [the longest x1 6.32 us: shards(): lax.all_to_all(key_split, 'seq', split_axis=2, concat_axis=1, tiled=True)]
    while x48 -> x0, local copies, waits for them, and re-layouts: 23.4 us -> none  [the longest x12 10 us: slot_data(): scores = lax.dynamic_index_in_dim(scores_all, position, 0, keepdims=False)]
    gather x32 -> x0, local copies, waits for them, and re-layouts: 20.4 us -> none  [the longest x12 8.96 us: accumulate(): values = jnp.take(value_blk, blocks, axis=0)]
  transfers between devices with their start and end apart: 7 -> 12, of which waited for: 6 -> 5; matrix products, arithmetic and copies ran while one was open for 24% -> 0% of each run, Pallas kernels for 0% -> 8%
where the time goes in v1:
time: 91.5 us; the launch traced here: 91.1 us
  starting transfers between devices  46.3 us (51%)
  waiting for transfers between devices  31.2 us (34%)
  Pallas kernels  8.65 us (9%)
  local copies, waits for them, and re-layouts  4.17 us (5%)
    ppermute x6, starting transfers between devices, shards(): lax.ppermute(outs[s], 'seq', [(j, (j - s) % size) for j in range(size)])  35.7 us
    ppermute x6, waiting for transfers between devices, shards(): lax.ppermute(outs[s], 'seq', [(j, (j - s) % size) for j in range(size)])  18.6 us
    ppermute x6, waiting for transfers between devices, shards(): lax.ppermute(packed[s - 1], 'seq', [(j, (j + s) % size) for j in range(si...  12.6 us
    ppermute x6, starting transfers between devices, shards(): lax.ppermute(packed[s - 1], 'seq', [(j, (j + s) % size) for j in range(si...  10.6 us
    pallas_call x2, Pallas kernels, run_heads(): pl.pallas_call(functools.partial(heads_kernel, size, heads, first, block)...  6.56 us
    unnamed x12, local copies, waits for them, and re-layouts  4.17 us
  transfers between devices with their start and end apart: 12, of which 5 were waited for; matrix products, arithmetic and copies ran while one was open for 0% of the time, Pallas kernels for 8%

profile of v1, /device:TPU:0, one launch (start us, length us, event | category | flops | bytes accessed | tf_op | source)
XLA Modules:
  0.0 91.1 jit_solution(16730823338776739948)
XLA Ops:
  0.6 0.0 copy-start
  0.6 1.0 %copy-done = bf16[1,128,2048]{2,1,0:T(8,128)(2,1)S(1)} copy-done((bf16[1,128,2048]{2,1,0:T(8,128)(2,1)S(1)}, bf16[1,128,2048]{2,1,0:T(8,128)(2,1)}, u32[]{:S(2)}) %copy-start) | copy-done | bytes 524312
  1.7 0.0 copy-start.1
  1.7 1.0 %copy-done.1 = bf16[1,128,2048]{2,1,0:T(8,128)(2,1)S(1)} copy-done((bf16[1,128,2048]{2,1,0:T(8,128)(2,1)S(1)}, bf16[1,128,2048]{2,1,0:T(8,128)(2,1)}, u32[]{:S(2)}) %copy-start.1) | copy-done | bytes 524312
  2.7 0.0 copy-start.2
  2.7 1.0 %copy-done.2 = bf16[1,128,2048]{2,1,0:T(8,128)(2,1)S(1)} copy-done((bf16[1,128,2048]{2,1,0:T(8,128)(2,1)S(1)}, bf16[1,128,2048]{2,1,0:T(8,128)(2,1)}, u32[]{:S(2)}) %copy-start.2) | copy-done | bytes 524312
  3.8 0.0 copy-start.3
  3.8 1.0 %copy-done.3 = bf16[1,128,2048]{2,1,0:T(8,128)(2,1)S(1)} copy-done((bf16[1,128,2048]{2,1,0:T(8,128)(2,1)S(1)}, bf16[1,128,2048]{2,1,0:T(8,128)(2,1)}, u32[]{:S(2)}) %copy-start.3) | copy-done | bytes 524312
  4.8 0.3 pack.2
  5.1 3.1 %collective-permute-start = (bf16[4,128,256]{2,1,0:T(8,128)(2,1)S(1)}, bf16[4,128,256]{2,1,0:T(8,128)(2,1)S(1)}, u32[]{:S(2)}, u32[]{:S(2)}) collective-permute-start(bf16[4,128,256]{2,1,0:T(8,128)(2,1)S(1)} %get-tuple-element.17), channel_id=1, source_target_pairs={{0,4},{4,8},{8,12},{12,0},{1,5},{5,9},{9,13},{13,1},{2,6},{6,10},{... | collective-permute-start | bytes 786440 | tf_op jit(solution)/shard_map/ppermute | solution.py:252
  8.2 2.6 %collective-permute-start.1 = (bf16[4,128,256]{2,1,0:T(8,128)(2,1)S(1)}, bf16[4,128,256]{2,1,0:T(8,128)(2,1)S(1)}, u32[]{:S(2)}, u32[]{:S(2)}) collective-permute-start(bf16[4,128,256]{2,1,0:T(8,128)(2,1)S(1)} %get-tuple-element.18), channel_id=1, source_target_pairs={{0,8},{4,12},{8,0},{12,4},{1,9},{5,13},{9,1},{13,5},{2,10},{6,14},... | collective-permute-start | bytes 786440 | tf_op jit(solution)/shard_map/ppermute | solution.py:252
  10.8 1.3 %collective-permute-start.2 = (bf16[4,128,256]{2,1,0:T(8,128)(2,1)S(1)}, bf16[4,128,256]{2,1,0:T(8,128)(2,1)S(1)}, u32[]{:S(2)}, u32[]{:S(2)}) collective-permute-start(bf16[4,128,256]{2,1,0:T(8,128)(2,1)S(1)} %get-tuple-element.19), channel_id=1, source_target_pairs={{0,12},{4,0},{8,4},{12,8},{1,13},{5,1},{9,5},{13,9},{2,14},{6,2},{... | collective-permute-start | bytes 786440 | tf_op jit(solution)/shard_map/ppermute | solution.py:252
  12.2 0.0 copy-start.5
  12.2 0.3 pack.3
  12.5 0.0 copy-start.4
  12.5 0.7 collective-permute-start.6
  13.2 0.3 collective-permute-start.7
  13.6 0.0 copy-done.5
  13.6 0.1 iota_compare_fusion.1
  13.7 3.9 %collective-permute-done.refs_4_ = bf16[4,128,256]{2,1,0:T(8,128)(2,1)S(1)} collective-permute-done((bf16[4,128,256]{2,1,0:T(8,128)(2,1)S(1)}, bf16[4,128,256]{2,1,0:T(8,128)(2,1)S(1)}, u32[]{:S(2)}, u32[]{:S(2)}) %collective-permute-start) | collective-permute-done | bytes 262176 | tf_op jit(solution)/shard_map/ppermute | solution.py:252
  17.5 2.5 %collective-permute-start.8 = (bf16[4,128,256]{2,1,0:T(8,128)(2,1)S(1)}, bf16[4,128,256]{2,1,0:T(8,128)(2,1)S(1)}, u32[]{:S(2)}, u32[]{:S(2)}) collective-permute-start(bf16[4,128,256]{2,1,0:T(8,128)(2,1)S(1)} %get-tuple-element.26), channel_id=1, source_target_pairs={{0,12},{4,0},{8,4},{12,8},{1,13},{5,1},{9,5},{13,9},{2,14},{6,2},{... | collective-permute-start | bytes 786440 | tf_op jit(solution)/shard_map/ppermute | solution.py:252
  20.0 0.0 copy-done.4
  20.0 0.1 select_reduce_fusion.uses
  20.1 8.7 %collective-permute-done.1.refs_5_ = bf16[4,128,256]{2,1,0:T(8,128)(2,1)S(1)} collective-permute-done((bf16[4,128,256]{2,1,0:T(8,128)(2,1)S(1)}, bf16[4,128,256]{2,1,0:T(8,128)(2,1)S(1)}, u32[]{:S(2)}, u32[]{:S(2)}) %collective-permute-start.1) | collective-permute-done | bytes 262176 | tf_op jit(solution)/shard_map/ppermute | solution.py:252
  28.8 0.0 collective-permute-done.2.refs_6_
  28.8 3.3 %heads.2 = (bf16[3,128,256]{2,1,0:T(8,128)(2,1)S(1)}, bf16[3,128,256]{2,1,0:T(8,128)(2,1)S(1)}, bf16[3,128,256]{2,1,0:T(8,128)(2,1)S(1)}, bf16[3,128,256]{2,1,0:T(8,128)(2,1)S(1)}) custom-call(s32[1]{0:T(128)} %bitcast.place, f32[4,4,4]{2,1,0:T(4,128)S(1)} %select_reduce_fusion.uses, bf16[1,128,2048]{2,1,0:T(8,128)(2,1)S(1)} %copy-done, ...), custom_call_target="tpu_custom_call" | custom-call | flops 671088640 | bytes 1835008 | tf_op jit(solution)/shard_map/heads/pallas_call | solution.py:152
  32.1 20.8 %collective-permute-start.3 = (bf16[3,128,256]{2,1,0:T(8,128)(2,1)S(1)}, bf16[3,128,256]{2,1,0:T(8,128)(2,1)S(1)}, u32[]{:S(2)}, u32[]{:S(2)}) collective-permute-start(bf16[3,128,256]{2,1,0:T(8,128)(2,1)S(1)} %get-tuple-element.21), channel_id=1, source_target_pairs={{0,12},{4,0},{8,4},{12,8},{1,13},{5,1},{9,5},{13,9},{2,14},{6,2},{... | collective-permute-start | bytes 589832 | tf_op jit(solution)/shard_map/ppermute | solution.py:258
  52.9 0.0 collective-permute-start.4
  52.9 0.0 collective-permute-done.6.refs_4_
  52.9 1.6 %collective-permute-start.5 = (bf16[3,128,256]{2,1,0:T(8,128)(2,1)S(1)}, bf16[3,128,256]{2,1,0:T(8,128)(2,1)S(1)}, u32[]{:S(2)}, u32[]{:S(2)}) collective-permute-start(bf16[3,128,256]{2,1,0:T(8,128)(2,1)S(1)} %get-tuple-element.23), channel_id=1, source_target_pairs={{0,4},{4,8},{8,12},{12,0},{1,5},{5,9},{9,13},{13,1},{2,6},{6,10},{... | collective-permute-start | bytes 589832 | tf_op jit(solution)/shard_map/ppermute | solution.py:258
  54.5 0.0 collective-permute-done.7.refs_5_
  54.5 0.0 collective-permute-done.8.refs_6_
  54.5 3.3 %heads.3 = (bf16[3,128,256]{2,1,0:T(8,128)(2,1)S(1)}, bf16[3,128,256]{2,1,0:T(8,128)(2,1)S(1)}, bf16[3,128,256]{2,1,0:T(8,128)(2,1)S(1)}, bf16[3,128,256]{2,1,0:T(8,128)(2,1)S(1)}) custom-call(s32[1]{0:T(128)} %bitcast.place, f32[4,4,4]{2,1,0:T(4,128)S(1)} %select_reduce_fusion.uses, bf16[1,128,2048]{2,1,0:T(8,128)(2,1)S(1)} %copy-done, ...), custom_call_target="tpu_custom_call" | custom-call | flops 671088640 | bytes 1835008 | tf_op jit(solution)/shard_map/heads/pallas_call | solution.py:152
  57.8 12.7 %collective-permute-start.9 = (bf16[3,128,256]{2,1,0:T(8,128)(2,1)S(1)}, bf16[3,128,256]{2,1,0:T(8,128)(2,1)S(1)}, u32[]{:S(2)}, u32[]{:S(2)}) collective-permute-start(bf16[3,128,256]{2,1,0:T(8,128)(2,1)S(1)} %get-tuple-element.28), channel_id=1, source_target_pairs={{0,12},{4,0},{8,4},{12,8},{1,13},{5,1},{9,5},{13,9},{2,14},{6,2},{... | collective-permute-start | bytes 589832 | tf_op jit(solution)/shard_map/ppermute | solution.py:258
  70.5 0.0 collective-permute-start.10
  70.5 0.0 collective-permute-done.3.refs_1_
  70.5 0.6 collective-permute-start.11
  71.1 4.1 %collective-permute-done.4.refs_2_ = bf16[3,128,256]{2,1,0:T(8,128)(2,1)S(1)} collective-permute-done((bf16[3,128,256]{2,1,0:T(8,128)(2,1)S(1)}, bf16[3,128,256]{2,1,0:T(8,128)(2,1)S(1)}, u32[]{:S(2)}, u32[]{:S(2)}) %collective-permute-start.4) | collective-permute-done | bytes 196640 | tf_op jit(solution)/shard_map/ppermute | solution.py:258
  75.2 0.0 collective-permute-done.5.refs_3_
  75.2 3.8 %collective-permute-done.9.refs_5_ = bf16[3,128,256]{2,1,0:T(8,128)(2,1)S(1)} collective-permute-done((bf16[3,128,256]{2,1,0:T(8,128)(2,1)S(1)}, bf16[3,128,256]{2,1,0:T(8,128)(2,1)S(1)}, u32[]{:S(2)}, u32[]{:S(2)}) %collective-permute-start.9) | collective-permute-done | bytes 196640 | tf_op jit(solution)/shard_map/ppermute | solution.py:258
  79.0 10.7 %collective-permute-done.10.refs_6_ = bf16[3,128,256]{2,1,0:T(8,128)(2,1)S(1)} collective-permute-done((bf16[3,128,256]{2,1,0:T(8,128)(2,1)S(1)}, bf16[3,128,256]{2,1,0:T(8,128)(2,1)S(1)}, u32[]{:S(2)}, u32[]{:S(2)}) %collective-permute-start.10) | collective-permute-done | bytes 196640 | tf_op jit(solution)/shard_map/ppermute | solution.py:258
  89.7 0.0 collective-permute-done.11.refs_7_
  89.7 1.4 %put_in_place.1 = (bf16[1,128,2048]{2,1,0:T(8,128)(2,1)}, bf16[1,128,2048]{2,1,0:T(8,128)(2,1)}, bf16[1,128,2048]{2,1,0:T(8,128)(2,1)}) custom-call(s32[1]{0:T(128)} %bitcast.place, bf16[3,128,256]{2,1,0:T(8,128)(2,1)S(1)} %get-tuple-element.20.refs_0_, bf16[3,128,256]{2,1,0:T(8,128)(2,1)S(1)} %collective-permute-done.3.refs_1_, ...), custom_call_target="tpu_custom_call" | custom-call | tf_op jit(solution)/shard_map/put_in_place/pallas_call | solution.py:217
Async XLA Ops:
  0.6 1.0 %copy-start = (bf16[1,128,2048]{2,1,0:T(8,128)(2,1)S(1)}, bf16[1,128,2048]{2,1,0:T(8,128)(2,1)}, u32[]{:S(2)}) copy-start(bf16[1,128,2048]{2,1,0:T(8,128)(2,1)} %refs_0_.7) | copy-start | bytes 1572868
  1.7 1.0 %copy-start.1 = (bf16[1,128,2048]{2,1,0:T(8,128)(2,1)S(1)}, bf16[1,128,2048]{2,1,0:T(8,128)(2,1)}, u32[]{:S(2)}) copy-start(bf16[1,128,2048]{2,1,0:T(8,128)(2,1)} %refs_1_.7) | copy-start | bytes 1572868
  2.7 1.0 %copy-start.2 = (bf16[1,128,2048]{2,1,0:T(8,128)(2,1)S(1)}, bf16[1,128,2048]{2,1,0:T(8,128)(2,1)}, u32[]{:S(2)}) copy-start(bf16[1,128,2048]{2,1,0:T(8,128)(2,1)} %refs_2_.7) | copy-start | bytes 1572868
  3.8 1.0 %copy-start.3 = (bf16[1,128,2048]{2,1,0:T(8,128)(2,1)S(1)}, bf16[1,128,2048]{2,1,0:T(8,128)(2,1)}, u32[]{:S(2)}) copy-start(bf16[1,128,2048]{2,1,0:T(8,128)(2,1)} %refs_3_.7) | copy-start | bytes 1572868
  5.1 12.4 %collective-permute-start = (bf16[4,128,256]{2,1,0:T(8,128)(2,1)S(1)}, bf16[4,128,256]{2,1,0:T(8,128)(2,1)S(1)}, u32[]{:S(2)}, u32[]{:S(2)}) collective-permute-start(bf16[4,128,256]{2,1,0:T(8,128)(2,1)S(1)} %get-tuple-element.17), channel_id=1, source_target_pairs={{0,4},{4,8},{8,12},{12,0},{1,5},{5,9},{9,13},{13,1},{2,6},{6,10},{... | collective-permute-start | bytes 786440 | tf_op jit(solution)/shard_map/ppermute | solution.py:252
  8.2 20.6 %collective-permute-start.1 = (bf16[4,128,256]{2,1,0:T(8,128)(2,1)S(1)}, bf16[4,128,256]{2,1,0:T(8,128)(2,1)S(1)}, u32[]{:S(2)}, u32[]{:S(2)}) collective-permute-start(bf16[4,128,256]{2,1,0:T(8,128)(2,1)S(1)} %get-tuple-element.18), channel_id=1, source_target_pairs={{0,8},{4,12},{8,0},{12,4},{1,9},{5,13},{9,1},{13,5},{2,10},{6,14},... | collective-permute-start | bytes 786440 | tf_op jit(solution)/shard_map/ppermute | solution.py:252
  10.8 18.0 %collective-permute-start.2 = (bf16[4,128,256]{2,1,0:T(8,128)(2,1)S(1)}, bf16[4,128,256]{2,1,0:T(8,128)(2,1)S(1)}, u32[]{:S(2)}, u32[]{:S(2)}) collective-permute-start(bf16[4,128,256]{2,1,0:T(8,128)(2,1)S(1)} %get-tuple-element.19), channel_id=1, source_target_pairs={{0,12},{4,0},{8,4},{12,8},{1,13},{5,1},{9,5},{13,9},{2,14},{6,2},{... | collective-permute-start | bytes 786440 | tf_op jit(solution)/shard_map/ppermute | solution.py:252
  12.2 1.4 %copy-start.5 = (s32[4,4]{1,0:T(4,128)S(1)}, s32[4,4]{1,0:T(4,128)}, u32[]{:S(2)}) copy-start(s32[4,4]{1,0:T(4,128)} %param.11) | copy-start | bytes 196
  12.5 7.5 %copy-start.4 = (s32[4,4,6]{2,1,0:T(4,128)S(1)}, s32[4,4,6]{2,1,0:T(4,128)}, u32[]{:S(2)}) copy-start(s32[4,4,6]{2,1,0:T(4,128)} %param.10) | copy-start | bytes 1156
  12.5 40.4 %collective-permute-start.6 = (bf16[4,128,256]{2,1,0:T(8,128)(2,1)S(1)}, bf16[4,128,256]{2,1,0:T(8,128)(2,1)S(1)}, u32[]{:S(2)}, u32[]{:S(2)}) collective-permute-start(bf16[4,128,256]{2,1,0:T(8,128)(2,1)S(1)} %get-tuple-element.24), channel_id=1, source_target_pairs={{0,4},{4,8},{8,12},{12,0},{1,5},{5,9},{9,13},{13,1},{2,6},{6,10},{... | collective-permute-start | bytes 786440 | tf_op jit(solution)/shard_map/ppermute | solution.py:252
  13.2 41.2 %collective-permute-start.7 = (bf16[4,128,256]{2,1,0:T(8,128)(2,1)S(1)}, bf16[4,128,256]{2,1,0:T(8,128)(2,1)S(1)}, u32[]{:S(2)}, u32[]{:S(2)}) collective-permute-start(bf16[4,128,256]{2,1,0:T(8,128)(2,1)S(1)} %get-tuple-element.25), channel_id=1, source_target_pairs={{0,8},{4,12},{8,0},{12,4},{1,9},{5,13},{9,1},{13,5},{2,10},{6,14},... | collective-permute-start | bytes 786440 | tf_op jit(solution)/shard_map/ppermute | solution.py:252
  17.5 37.0 %collective-permute-start.8 = (bf16[4,128,256]{2,1,0:T(8,128)(2,1)S(1)}, bf16[4,128,256]{2,1,0:T(8,128)(2,1)S(1)}, u32[]{:S(2)}, u32[]{:S(2)}) collective-permute-start(bf16[4,128,256]{2,1,0:T(8,128)(2,1)S(1)} %get-tuple-element.26), channel_id=1, source_target_pairs={{0,12},{4,0},{8,4},{12,8},{1,13},{5,1},{9,5},{13,9},{2,14},{6,2},{... | collective-permute-start | bytes 786440 | tf_op jit(solution)/shard_map/ppermute | solution.py:252
  32.1 38.4 %collective-permute-start.3 = (bf16[3,128,256]{2,1,0:T(8,128)(2,1)S(1)}, bf16[3,128,256]{2,1,0:T(8,128)(2,1)S(1)}, u32[]{:S(2)}, u32[]{:S(2)}) collective-permute-start(bf16[3,128,256]{2,1,0:T(8,128)(2,1)S(1)} %get-tuple-element.21), channel_id=1, source_target_pairs={{0,12},{4,0},{8,4},{12,8},{1,13},{5,1},{9,5},{13,9},{2,14},{6,2},{... | collective-permute-start | bytes 589832 | tf_op jit(solution)/shard_map/ppermute | solution.py:258
  52.9 22.3 %collective-permute-start.4 = (bf16[3,128,256]{2,1,0:T(8,128)(2,1)S(1)}, bf16[3,128,256]{2,1,0:T(8,128)(2,1)S(1)}, u32[]{:S(2)}, u32[]{:S(2)}) collective-permute-start(bf16[3,128,256]{2,1,0:T(8,128)(2,1)S(1)} %get-tuple-element.22), channel_id=1, source_target_pairs={{0,8},{4,12},{8,0},{12,4},{1,9},{5,13},{9,1},{13,5},{2,10},{6,14},... | collective-permute-start | bytes 589832 | tf_op jit(solution)/shard_map/ppermute | solution.py:258
  52.9 22.3 %collective-permute-start.5 = (bf16[3,128,256]{2,1,0:T(8,128)(2,1)S(1)}, bf16[3,128,256]{2,1,0:T(8,128)(2,1)S(1)}, u32[]{:S(2)}, u32[]{:S(2)}) collective-permute-start(bf16[3,128,256]{2,1,0:T(8,128)(2,1)S(1)} %get-tuple-element.23), channel_id=1, source_target_pairs={{0,4},{4,8},{8,12},{12,0},{1,5},{5,9},{9,13},{13,1},{2,6},{6,10},{... | collective-permute-start | bytes 589832 | tf_op jit(solution)/shard_map/ppermute | solution.py:258
  57.8 21.2 %collective-permute-start.9 = (bf16[3,128,256]{2,1,0:T(8,128)(2,1)S(1)}, bf16[3,128,256]{2,1,0:T(8,128)(2,1)S(1)}, u32[]{:S(2)}, u32[]{:S(2)}) collective-permute-start(bf16[3,128,256]{2,1,0:T(8,128)(2,1)S(1)} %get-tuple-element.28), channel_id=1, source_target_pairs={{0,12},{4,0},{8,4},{12,8},{1,13},{5,1},{9,5},{13,9},{2,14},{6,2},{... | collective-permute-start | bytes 589832 | tf_op jit(solution)/shard_map/ppermute | solution.py:258
  70.5 19.3 %collective-permute-start.10 = (bf16[3,128,256]{2,1,0:T(8,128)(2,1)S(1)}, bf16[3,128,256]{2,1,0:T(8,128)(2,1)S(1)}, u32[]{:S(2)}, u32[]{:S(2)}) collective-permute-start(bf16[3,128,256]{2,1,0:T(8,128)(2,1)S(1)} %get-tuple-element.29), channel_id=1, source_target_pairs={{0,8},{4,12},{8,0},{12,4},{1,9},{5,13},{9,1},{13,5},{2,10},{6,14},... | collective-permute-start | bytes 589832 | tf_op jit(solution)/shard_map/ppermute | solution.py:258
  70.5 19.3 %collective-permute-start.11 = (bf16[3,128,256]{2,1,0:T(8,128)(2,1)S(1)}, bf16[3,128,256]{2,1,0:T(8,128)(2,1)S(1)}, u32[]{:S(2)}, u32[]{:S(2)}) collective-permute-start(bf16[3,128,256]{2,1,0:T(8,128)(2,1)S(1)} %get-tuple-element.30), channel_id=1, source_target_pairs={{0,4},{4,8},{8,12},{12,0},{1,5},{5,9},{9,13},{13,1},{2,6},{6,10},{... | collective-permute-start | bytes 589832 | tf_op jit(solution)/shard_map/ppermute | solution.py:258
